TPU v7x, 256 devices: a whole 4x4x8 slice. The times are simulated.
256 devices in a mesh: dp: 16 (over x, z_lo), tensor: 16 (over y, z_hi, core).
Axes of the slice: x: 4, y: 4, z: 8 (z_hi: 2, z_lo: 4; z = z_hi * 4 + z_lo), core: 2. Of those that a mesh axis runs over, the one named last changes fastest.
Arguments:
- tokens: bfloat16 [6144, 2048], P('dp', 'tensor'), may hold values from -6 to 6
- cotangent: bfloat16 [6144, 2048], P('dp', 'tensor'), may hold values from -6 to 6
- prefix: int32 [48], P('dp'), may hold values from 2048 to 16384, as said below
- gate_weight: bfloat16 [2048, 16384], P('dp', 'tensor'), may hold values from -0.125 to 0.125
- up_weight: bfloat16 [2048, 16384], P('dp', 'tensor'), may hold values from -0.125 to 0.125
- down_weight: bfloat16 [16384, 2048], P('tensor', 'dp'), may hold values from -0.046875 to 0.046875
Outputs:
- mixed: bfloat16 [6144, 2048], P('dp', 'tensor')
- input_grad: bfloat16 [6144, 2048], P('dp', 'tensor')
- gate_grad: bfloat16 [2048, 16384], P('dp', 'tensor')
- up_grad: bfloat16 [2048, 16384], P('dp', 'tensor')
- down_grad: bfloat16 [16384, 2048], P('tensor', 'dp')
Inputs may be any that keep to these rules, and one draw needn't show every extreme that they name: `prefix`: every entry is 2048, 4096, 8192 or 16384.
All inputs are finite; a program needn't handle non-finite values.
Results may differ from a plain program's by a relative error of at most 0.02.
Values may be sent and summed in bfloat16 or wider, within the bound.
No kernel may reach another device: no remote copies, remote signals or barrier semaphores. Data moves between devices by JAX's collectives and lax.ppermute only.
A program may use at most 128 MiB of HBM per device.

v0:
```python
import math

import jax
import jax.numpy as jnp
from jax import lax
from jax.sharding import PartitionSpec as P

GROUP = 128


def local_terms(inputs, cotangent_rows, keep_mask, gate_full, up_full, down_full):
    gate_pre = jnp.dot(inputs, gate_full, preferred_element_type=jnp.float32)
    up_pre = jnp.dot(inputs, up_full, preferred_element_type=jnp.float32)
    gate_sig = jax.nn.sigmoid(gate_pre)
    gate_act = gate_pre * gate_sig
    hidden = jnp.where(keep_mask, gate_act * up_pre, 0.0).astype(jnp.bfloat16)
    grad_hidden = lax.dot_general(
        cotangent_rows, down_full, (((1,), (1,)), ((), ())), preferred_element_type=jnp.float32
    )
    grad_gate = jnp.where(
        keep_mask, grad_hidden * up_pre * gate_sig * (1.0 + gate_pre * (1.0 - gate_sig)), 0.0
    ).astype(jnp.bfloat16)
    grad_upper = jnp.where(keep_mask, grad_hidden * gate_act, 0.0).astype(jnp.bfloat16)
    return (hidden, grad_gate, grad_upper)


def local(tokens, cotangent, prefix, gate_weight, up_weight, down_weight):
    row_count = tokens.shape[0]
    grad_scale = 1.0 / math.sqrt(row_count * lax.axis_size("dp"))
    whole_in, whole_cot = (
        lax.all_gather(tokens, "tensor", axis=1, tiled=True),
        lax.all_gather(cotangent, "tensor", axis=1, tiled=True),
    )
    gate_full, up_full = (
        lax.all_gather(gate_weight, "dp", axis=0, tiled=True),
        lax.all_gather(up_weight, "dp", axis=0, tiled=True),
    )
    down_full = lax.all_gather(down_weight, "dp", axis=1, tiled=True)
    unit_count = gate_full.shape[1]
    first_unit = lax.axis_index("tensor") * unit_count
    unit_ids = first_unit + jnp.arange(unit_count, dtype=jnp.int32)
    keep_mask = unit_ids[None, :] < jnp.repeat(prefix, GROUP)[:, None]
    hidden, grad_gate, grad_upper = local_terms(
        whole_in, whole_cot, keep_mask, gate_full, up_full, down_full
    )
    contract_rows = (((0,), (0,)), ((), ()))
    out_terms = jnp.dot(hidden, down_full, preferred_element_type=jnp.float32)
    mixed = lax.psum_scatter(
        out_terms.astype(jnp.bfloat16), "tensor", scatter_dimension=1, tiled=True
    )
    term_down = (
        lax.dot_general(hidden, whole_cot, contract_rows, preferred_element_type=jnp.float32)
        * grad_scale
    )
    back_gate = lax.dot_general(
        grad_gate, gate_full, (((1,), (1,)), ((), ())), preferred_element_type=jnp.float32
    )
    back_up = lax.dot_general(
        grad_upper, up_full, (((1,), (1,)), ((), ())), preferred_element_type=jnp.float32
    )
    input_grad = lax.psum_scatter(
        (back_gate + back_up).astype(jnp.bfloat16), "tensor", scatter_dimension=1, tiled=True
    )
    term_gate = (
        lax.dot_general(whole_in, grad_gate, contract_rows, preferred_element_type=jnp.float32)
        * grad_scale
    )
    term_up = (
        lax.dot_general(whole_in, grad_upper, contract_rows, preferred_element_type=jnp.float32)
        * grad_scale
    )
    summed_gate, summed_up, summed_down = (
        lax.psum_scatter(
            term_gate.astype(jnp.bfloat16), "dp", scatter_dimension=0, tiled=True
        ).astype(jnp.float32),
        lax.psum_scatter(
            term_up.astype(jnp.bfloat16), "dp", scatter_dimension=0, tiled=True
        ).astype(jnp.float32),
        lax.psum_scatter(
            term_down.astype(jnp.bfloat16), "dp", scatter_dimension=1, tiled=True
        ).astype(jnp.float32),
    )
    down_grad = summed_down.astype(jnp.bfloat16)
    return (
        mixed,
        input_grad,
        summed_gate.astype(jnp.bfloat16),
        summed_up.astype(jnp.bfloat16),
        down_grad,
    )


def solution(mesh):
    return jax.shard_map(
        local,
        mesh=mesh,
        in_specs=(
            P("dp", "tensor"),
            P("dp", "tensor"),
            P("dp"),
            P("dp", "tensor"),
            P("dp", "tensor"),
            P("tensor", "dp"),
        ),
        out_specs=(
            P("dp", "tensor"),
            P("dp", "tensor"),
            P("dp", "tensor"),
            P("dp", "tensor"),
            P("tensor", "dp"),
        ),
        check_vma=False,
    )
```

profile of v0, /device:TPU:10, one launch (start us, length us, event | category | flops | bytes accessed | tf_op | source)
XLA Modules:
  0.0 934.8 jit_solution(6868664519020328215)
XLA Ops:
  10.7 62.0 %all-gather.6.cloned.1.call-done = bf16[384,2048]{1,0:T(8,128)(2,1)} async-done(((bf16[384,128]{1,0:T(8,128)(2,1)}), bf16[384,2048]{1,0:T(8,128)(2,1)}) %all-gather.6.cloned.1.call-update) | async-done | bytes 1572880 | tf_op jit(solution)/shard_map/all_gather | solution.py:31
  72.7 97.8 %all-gather.10.cloned.1.call-done = bf16[2048,1024]{1,0:T(8,128)(2,1)} async-done(((bf16[128,1024]{1,0:T(8,128)(2,1)}), bf16[2048,1024]{1,0:T(8,128)(2,1)}) %all-gather.10.cloned.1.call-update) | async-done | bytes 4194320 | tf_op jit(solution)/shard_map/all_gather | solution.py:36
  170.5 5.6 fusion.7
  176.1 95.4 %all-gather.8.cloned.1.call-done = bf16[2048,1024]{1,0:T(8,128)(2,1)} async-done(((bf16[128,1024]{1,0:T(8,128)(2,1)}), bf16[2048,1024]{1,0:T(8,128)(2,1)}) %all-gather.8.cloned.1.call-update) | async-done | bytes 4194320 | tf_op jit(solution)/shard_map/all_gather | solution.py:35
  271.5 5.2 fusion.6
  276.7 55.9 %all-gather.14.cloned.1.call-done = bf16[384,2048]{1,0:T(8,128)(2,1)} async-done(((bf16[384,128]{1,0:T(8,128)(2,1)}), bf16[384,2048]{1,0:T(8,128)(2,1)}) %all-gather.14.cloned.1.call-update) | async-done | bytes 1572880 | tf_op jit(solution)/shard_map/all_gather | solution.py:32
  332.6 109.4 %all-gather.12.cloned.1.call-done = bf16[1024,2048]{1,0:T(8,128)(2,1)} async-done(((bf16[1024,128]{1,0:T(8,128)(2,1)}), bf16[1024,2048]{1,0:T(8,128)(2,1)}) %all-gather.12.cloned.1.call-update) | async-done | bytes 4194320 | tf_op jit(solution)/shard_map/all_gather | solution.py:38
  442.0 7.4 fusion.4
  449.4 0.9 copy-done.9
  450.3 1.8 convolution_convert_fusion
  452.1 1.6 copy.15
  453.8 1.1 copy-done.5
  454.9 4.2 fusion.8
  459.0 1.8 add_convert_fusion
  460.9 1.6 copy.17
  462.7 1.2 copy-done.4
  463.9 5.6 multiply_convert_fusion
  469.4 6.5 copy.23
  476.0 1.1 copy-done.8
  477.0 4.4 fusion.1
  481.4 6.5 copy.21
  488.0 1.1 copy-done.6
  489.0 4.3 fusion
  493.4 6.3 copy.19
  499.7 38.0 %reduce-scatter.16.cloned.1.call-done = bf16[128,384]{1,0:T(8,128)(2,1)} async-done(((bf16[2048,384]{1,0:T(8,128)(2,1)}), bf16[128,384]{1,0:T(8,128)(2,1)}) %reduce-scatter.16.cloned.1.call-update) | async-done | bytes 98320
  537.7 1.6 copy.16
  539.3 82.5 %reduce-scatter.18.cloned.1.call-done = bf16[128,384]{1,0:T(8,128)(2,1)} async-done(((bf16[2048,384]{1,0:T(8,128)(2,1)}), bf16[128,384]{1,0:T(8,128)(2,1)}) %reduce-scatter.18.cloned.1.call-update) | async-done | bytes 98320
  621.8 1.6 copy.18
  623.5 97.3 %reduce-scatter.24.cloned.1.call-done = bf16[128,1024]{1,0:T(8,128)(2,1)} async-done(((bf16[2048,1024]{1,0:T(8,128)(2,1)}), bf16[128,1024]{1,0:T(8,128)(2,1)}) %reduce-scatter.24.cloned.1.call-update) | async-done | bytes 262160
  720.8 1.8 copy.24
  722.6 101.7 %reduce-scatter.22.cloned.1.call-done = bf16[128,1024]{1,0:T(8,128)(2,1)} async-done(((bf16[2048,1024]{1,0:T(8,128)(2,1)}), bf16[128,1024]{1,0:T(8,128)(2,1)}) %reduce-scatter.22.cloned.1.call-update) | async-done | bytes 262160
  824.3 103.6 %reduce-scatter.20.cloned.1.call-done = bf16[128,1024]{1,0:T(8,128)(2,1)} async-done(((bf16[2048,1024]{1,0:T(8,128)(2,1)}), bf16[128,1024]{1,0:T(8,128)(2,1)}) %reduce-scatter.20.cloned.1.call-update) | async-done | bytes 262160
  (37 shorter events, 3.9 us)
Async XLA Ops:
  7.2 3.5 copy-start
  7.2 65.5 %all-gather.6.cloned.1.call-start = ((), (), s32[]{:S(2)}) async-start(), calls=%async_computation.5 | async-start | bytes 1671168 | tf_op jit(solution)/shard_map/all_gather | solution.py:31
  7.9 162.6 %all-gather.10.cloned.1.call-start = ((), (), s32[]{:S(2)}) async-start(), calls=%async_computation.7 | async-start | bytes 4456448 | tf_op jit(solution)/shard_map/all_gather | solution.py:36
  8.7 262.9 %all-gather.8.cloned.1.call-start = ((), (), s32[]{:S(2)}) async-start(), calls=%async_computation.6 | async-start | bytes 4456448 | tf_op jit(solution)/shard_map/all_gather | solution.py:35
  9.4 323.2 %all-gather.14.cloned.1.call-start = ((), (), s32[]{:S(2)}) async-start(), calls=%async_computation.9 | async-start | bytes 1671168 | tf_op jit(solution)/shard_map/all_gather | solution.py:32
  10.0 432.0 %all-gather.12.cloned.1.call-start = ((), (), s32[]{:S(2)}) async-start(), calls=%async_computation.8 | async-start | bytes 4456448 | tf_op jit(solution)/shard_map/all_gather | solution.py:38
  10.6 527.1 %reduce-scatter.16.cloned.1.call-start = ((), (), s32[]{:S(2)}) async-start(), calls=%async_computation.10 | async-start | bytes 1671168
  72.7 198.8 %copy-start.3 = (bf16[384,2048]{1,0:T(8,128)(2,1)S(1)}, bf16[384,2048]{1,0:T(8,128)(2,1)}, u32[]{:S(2)}) copy-start(bf16[384,2048]{1,0:T(8,128)(2,1)} %all-gather.6.cloned.1.call-done) | copy-start | bytes 4718596
  442.0 8.3 copy-start.2
  449.4 0.9 copy-start.9
  453.7 1.1 copy-start.5
  453.7 168.1 %reduce-scatter.18.cloned.1.call-start = ((), (), s32[]{:S(2)}) async-start(), calls=%async_computation.11 | async-start | bytes 1671168
  454.9 4.2 copy-start.1
  454.9 4.2 copy-start.7
  462.5 1.4 copy-start.4
  462.5 258.3 %reduce-scatter.24.cloned.1.call-start = ((), (), s32[]{:S(2)}) async-start(), calls=%async_computation.14 | async-start | bytes 4456448
  475.9 1.1 copy-start.8
  475.9 348.4 %reduce-scatter.22.cloned.1.call-start = ((), (), s32[]{:S(2)}) async-start(), calls=%async_computation.13 | async-start | bytes 4456448
  487.9 1.1 copy-start.6
  487.9 440.0 %reduce-scatter.20.cloned.1.call-start = ((), (), s32[]{:S(2)}) async-start(), calls=%async_computation.12 | async-start | bytes 4456448
Sparse Core Ops, SparseCore 0:
  10.6 62.1 all-gather.5
  74.5 95.9 all-gather.9
  172.3 99.1 all-gather.7
  273.9 58.6 all-gather.13
  334.2 107.7 all-gather.11
  453.9 83.7 reduce-scatter.15
  541.8 79.9 reduce-scatter.17
  624.4 96.3 reduce-scatter.23
  723.9 100.3 reduce-scatter.21
  827.3 100.5 reduce-scatter.19
where the time goes:
time: 939 us; the launch traced here: 935 us
  waiting for transfers between devices  847 us (90%)
  matrix products  40.3 us (4%)
  local copies, waits for them, and re-layouts  32.8 us (3%)
  between operations  14.2 us (2%)
    unnamed x15, waiting for transfers between devices  426 us
    all_gather x1, waiting for transfers between devices, local(): down_full = lax.all_gather(down_weight, 'dp', axis=1, tiled=True)  109 us
    all_gather x1, waiting for transfers between devices, local(): lax.all_gather(up_weight, 'dp', axis=0, tiled=True)  97.8 us
    all_gather x1, waiting for transfers between devices, local(): lax.all_gather(gate_weight, 'dp', axis=0, tiled=True)  95.4 us
    all_gather x1, waiting for transfers between devices, local(): lax.all_gather(tokens, 'tensor', axis=1, tiled=True)  62 us
    all_gather x1, waiting for transfers between devices, local(): lax.all_gather(cotangent, 'tensor', axis=1, tiled=True)  55.9 us
    unnamed x28, local copies, waits for them, and re-layouts  32.8 us
  transfers between devices with their start and end apart: 10, of which 10 were waited for; matrix products, arithmetic and copies ran while one was open for 6% of the time, Pallas kernels for 0%

commit v1 on v0

v1 whole, which is shorter than its diff:
```python
import math

import jax
import jax.numpy as jnp
from jax import lax
from jax.experimental import pallas as pl
from jax.experimental.pallas import tpu as pltpu
from jax.sharding import Mesh
from jax.sharding import PartitionSpec as P


D = 2048
TOK = 6144
BF = jnp.bfloat16
F32 = jnp.float32
HALF = 192
ROWS = 768
UNITS = 512
OFFS = (0, 1, -1, 2)
ZOFFS = (0, 1, -1, 2, -2, 3, -3, 4)
PARAMS = dict(vmem_limit_bytes=44 * 1024 * 1024)
ANY = pl.BlockSpec(memory_space=pl.ANY)
SMEM = pl.BlockSpec(memory_space=pltpu.SMEM)


def shift(value, axis, by):
    return lax.ppermute(value, axis, [(i, (i + by) % 4) for i in range(4)])


def shift_z(value, by):
    pairs = []
    for z in range(8):
        to = (z + by) % 8
        pairs.append(((z % 4) * 2 + z // 4, (to % 4) * 2 + to // 4))
    return lax.ppermute(value, ("zl", "zh"), pairs)


def swap(value):
    return lax.ppermute(value, "c", [(0, 1), (1, 0)])


def run_copies(copies, sems, first=0):
    started = []
    for n, (src, dst) in enumerate(copies):
        copy = pltpu.make_async_copy(src, dst, sems.at[first + n])
        copy.start()
        started.append(copy)
    return started


def wait_all(started):
    for copy in started:
        copy.wait()


def spot(value, step):
    return pl.ds(pl.multiple_of(value * step, step), step)


def cost(flops, size):
    return pl.CostEstimate(flops=int(flops), bytes_accessed=int(size), transcendentals=0)


def shape(*dims):
    return jax.ShapeDtypeStruct(dims, BF)


def pack_kernel(co, gate, up, down, *rest):
    outs, sems = rest[:3], rest[3]
    zl = co[1]
    copies = []
    for out, off in zip(outs, OFFS[1:]):
        to = lax.rem(zl + off + 4, 4)
        copies.append((gate.at[:, spot(to, 256)], out.at[:, pl.ds(0, 256)]))
        copies.append((up.at[:, spot(to, 256)], out.at[:, pl.ds(256, 256)]))
        for h in range(2):
            copies.append((down.at[spot(to * 2 + h, 128), :], out.at[:, pl.ds(512 + 128 * h, 128)]))
    wait_all(run_copies(copies, sems))


def place_kernel(co, gate, up, down, *rest):
    pieces, out, sems = rest[:3], rest[3], rest[4]
    zl = co[1]
    copies = [
        (gate.at[:, spot(zl, 256)], out.at[spot(zl, 128), pl.ds(0, 256)]),
        (up.at[:, spot(zl, 256)], out.at[spot(zl, 128), pl.ds(256, 256)]),
        (down.at[spot(zl, 256), :], out.at[pl.ds(512, 256), spot(zl, 128)]),
    ]
    for piece, off in zip(pieces, OFFS[1:]):
        at = lax.rem(zl - off + 4, 4)
        copies.append((piece.at[:, pl.ds(0, 512)], out.at[spot(at, 128), :]))
        for h in range(2):
            copies.append(
                (piece.at[:, pl.ds(512 + 128 * h, 128)], out.at[pl.ds(512 + 128 * h, 128), spot(at, 128)])
            )
    wait_all(run_copies(copies, sems))


def pack_back_kernel(co, total, *rest):
    outs, sems = rest[:3], rest[3]
    zl = co[1]
    copies = []
    for out, off in zip(outs, OFFS[1:]):
        to = lax.rem(zl + off + 4, 4)
        copies.append((total.at[spot(to, 128), :], out.at[:, pl.ds(0, 512)]))
        for h in range(2):
            copies.append(
                (total.at[pl.ds(512 + 128 * h, 128), spot(to, 128)], out.at[:, pl.ds(512 + 128 * h, 128)])
            )
    wait_all(run_copies(copies, sems))


def place_back_kernel(co, total, *rest):
    pieces, (gate, up, down), sems = rest[:3], rest[3:6], rest[6]
    zl = co[1]
    copies = [
        (total.at[spot(zl, 128), pl.ds(0, 256)], gate.at[:, spot(zl, 256)]),
        (total.at[spot(zl, 128), pl.ds(256, 256)], up.at[:, spot(zl, 256)]),
        (total.at[pl.ds(512, 256), spot(zl, 128)], down.at[spot(zl, 256), :]),
    ]
    for piece, off in zip(pieces, OFFS[1:]):
        at = lax.rem(zl - off + 4, 4)
        copies.append((piece.at[:, pl.ds(0, 256)], gate.at[:, spot(at, 256)]))
        copies.append((piece.at[:, pl.ds(256, 256)], up.at[:, spot(at, 256)]))
        for h in range(2):
            copies.append((piece.at[:, pl.ds(512 + 128 * h, 128)], down.at[spot(at * 2 + h, 128), :]))
    wait_all(run_copies(copies, sems))


def move(kernel, count, co, *args, out_shape):
    size = sum(a.size for a in args) * 2
    return pl.pallas_call(
        kernel,
        out_shape=out_shape,
        in_specs=[SMEM] + [ANY] * len(args),
        out_specs=jax.tree.map(lambda _: ANY, out_shape),
        scratch_shapes=[pltpu.SemaphoreType.DMA((count,))],
        cost_estimate=cost(0, size),
    )(co, *args)


def weight_copies(co, own, other, wide, down):
    x = co[0]
    gate_up, downs = [], []
    for half, group in enumerate((own, other)):
        for piece, off in zip(group, OFFS):
            at = lax.rem(x - off + 4, 4)
            if wide is not None:
                for part in range(2):
                    gate_up.append(
                        (
                            piece.at[pl.ds(0, 512), pl.ds(256 * part, 256)],
                            wide.at[spot(at, 512), pl.ds(512 * part + 256 * half, 256)],
                        )
                    )
            if down is not None:
                downs.append((piece.at[pl.ds(512, 256), :], down.at[pl.ds(256 * half, 256), spot(at, 512)]))
    return gate_up, downs


def token_copies(co, pieces, whole):
    y, z = co[2], co[5]
    copies = []
    for n, off in enumerate(ZOFFS):
        at = lax.rem(z - off + 8, 8)
        for o, y_off in enumerate(OFFS):
            ys = lax.rem(y - y_off + 4, 4)
            if n < 7:
                src = pieces[n].at[pl.ds(o * HALF, HALF), :]
            else:
                src = pieces[7 + o // 2].at[pl.ds((o % 2) * HALF, HALF), :]
            copies.append((src, whole.at[spot(lax.rem(at, 4), HALF), spot(ys * 2 + at // 4, 256)]))
    return copies


def cot_copies(co, pieces, whole):
    y, z = co[2], co[5]
    copies = []
    for o, y_off in enumerate(OFFS):
        ys = lax.rem(y - y_off + 4, 4)
        for n, off in enumerate(ZOFFS):
            at = lax.rem(z - off + 8, 8)
            src = pieces[o].at[pl.ds(n * HALF, HALF), :]
            copies.append((src, whole.at[spot(lax.rem(at, 4), HALF), spot(ys * 2 + at // 4, 256)]))
    return copies


NN = (((1,), (0,)), ((), ()))
NT = (((1,), (1,)), ((), ()))


def dot(a, b, dims):
    return lax.dot_general(a, b, dims, preferred_element_type=F32)


def hidden_kernel(co, *refs):
    tok_in, cot_in, w_own, w_other = refs[:9], refs[9:13], refs[13:17], refs[17:21]
    hid_out, grads_out, mixed_out = refs[21], refs[22], refs[23:32]
    tok, cot, wide, down, hid, grads, mixed, limits, sems = refs[32:]
    c, zl, y, zh, z = co[4], co[1], co[2], co[3], co[5]
    gate_up, downs = weight_copies(co, w_own, w_other, wide, down)
    limit_copies = []
    for n, off in enumerate(ZOFFS[:7]):
        if off in (0, 1, -1, 2):
            at = lax.rem(z - off + 8, 4)
            limit_copies.append((tok_in[n].at[pl.ds(ROWS, 16), :], limits.at[spot(at, 16), :]))
    early = run_copies(gate_up + token_copies(co, tok_in, tok) + limit_copies, sems)
    late = run_copies(cot_copies(co, cot_in, cot) + downs, sems, len(early))
    wait_all(early)
    wait_all(late)
    split = 128 - 64 * c
    for half in range(2):
        core = c if half == 0 else 1 - c
        first = ((y * 2 + zh) * 2 + core) * 1024 + zl * 256
        col = pl.ds(256 * half, 256)
        up_col = pl.ds(512 + 256 * half, 256)
        gate_pre = dot(tok[...], wide[:, col], NN)
        up_pre = dot(tok[...], wide[:, up_col], NN)
        grad_hidden = dot(cot[...], down[col, :], NT)
        unit = (first + lax.broadcasted_iota(jnp.int32, (HALF, 256), 1)).astype(F32)
        row = lax.broadcasted_iota(jnp.int32, (HALF, 256), 0)
        for block in range(4):
            rows = slice(block * HALF, block * HALF + HALF)
            low = limits[16 * block : 16 * block + 1, :].astype(F32)
            high = limits[16 * block + 1 : 16 * block + 2, :].astype(F32)
            keep = unit < jnp.where(row < split, low, high)
            g, u, gh = gate_pre[rows], up_pre[rows], grad_hidden[rows]
            sig = jax.nn.sigmoid(g)
            act = g * sig
            hid[rows, col] = jnp.where(keep, act * u, 0.0).astype(BF)
            grads[rows, col] = jnp.where(keep, gh * u * sig * (1.0 + g * (1.0 - sig)), 0.0).astype(BF)
            grads[rows, up_col] = jnp.where(keep, gh * act, 0.0).astype(BF)
    first_sem = len(early) + len(late)
    kept = run_copies([(hid, hid_out), (grads, grads_out)], sems, first_sem)

    @pl.loop(0, 8)
    def _(n):
        block = spot(n, 256)
        mixed[:, block] = dot(hid[...], down[:, block], NN).astype(BF)

    copies = []
    for n, off in enumerate(ZOFFS):
        to = lax.rem(z + off + 8, 8)
        for o, y_off in enumerate(OFFS):
            yd = lax.rem(y + y_off + 4, 4)
            src = mixed.at[spot(lax.rem(to, 4), HALF), spot(yd * 2 + to // 4, 256)]
            if n < 7:
                dst = mixed_out[n].at[pl.ds(o * HALF, HALF), :]
            else:
                dst = mixed_out[7 + o // 2].at[pl.ds((o % 2) * HALF, HALF), :]
            copies.append((src, dst))
    wait_all(run_copies(copies, sems, first_sem + 2))
    wait_all(kept)


def hidden_call(co, tok_in, cot_in, w_own, w_other):
    args = (*tok_in, *cot_in, *w_own, *w_other)
    outs = (
        [shape(ROWS, UNITS), shape(ROWS, 2 * UNITS)]
        + [shape(ROWS, 256) for _ in range(7)]
        + [shape(ROWS // 2, 256) for _ in range(2)]
    )
    out = pl.pallas_call(
        hidden_kernel,
        out_shape=outs,
        in_specs=[SMEM] + [ANY] * len(args),
        out_specs=[ANY] * len(outs),
        scratch_shapes=[
            pltpu.VMEM((ROWS, D), BF),
            pltpu.VMEM((ROWS, D), BF),
            pltpu.VMEM((D, 2 * UNITS), BF),
            pltpu.VMEM((UNITS, D), BF),
            pltpu.VMEM((ROWS, UNITS), BF),
            pltpu.VMEM((ROWS, 2 * UNITS), BF),
            pltpu.VMEM((ROWS, D), BF),
            pltpu.VMEM((64, 256), BF),
            pltpu.SemaphoreType.DMA((128 + 32,)),
        ],
        compiler_params=pltpu.CompilerParams(**PARAMS),
        cost_estimate=cost(8 * ROWS * D * UNITS, 18e6),
    )(co, *args)
    return out[0], out[1], out[2:]


def weight_grad_kernel(co, *refs):
    hid_in, grads_in, tok_in, cot_in = refs[0], refs[1], refs[2:11], refs[11:15]
    own_out, other_out = refs[15:19], refs[19:23]
    tok, cot, hid, grads, wide, down, hid_t, sems = refs[23:]
    scale = 1.0 / math.sqrt(TOK)
    first = run_copies([(grads_in, grads)] + token_copies(co, tok_in, tok), sems)
    second = run_copies([(hid_in, hid)] + cot_copies(co, cot_in, cot), sems, len(first))
    wait_all(first)
    wait_all(second)

    @pl.loop(0, 8)
    def _(n):
        block = spot(n, 256)
        turned = tok[:, block].T
        wide[block, :] = (dot(turned, grads[...], NN) * scale).astype(BF)

    hid_t[...] = hid[...].T

    @pl.loop(0, 8)
    def _(n):
        block = spot(n, 256)
        down[:, block] = (dot(hid_t[...], cot[:, block], NN) * scale).astype(BF)

    x = co[0]
    copies = []
    for half, group in enumerate((own_out, other_out)):
        for piece, off in zip(group, OFFS):
            to = lax.rem(x + off + 4, 4)
            for part in range(2):
                copies.append(
                    (
                        wide.at[spot(to, 512), pl.ds(512 * part + 256 * half, 256)],
                        piece.at[pl.ds(0, 512), pl.ds(256 * part, 256)],
                    )
                )
            copies.append((down.at[pl.ds(256 * half, 256), spot(to, 512)], piece.at[pl.ds(512, 256), :]))
    wait_all(run_copies(copies, sems, len(first) + len(second)))


def weight_grad_call(co, hid, grads, tok_in, cot_in):
    args = (hid, grads, *tok_in, *cot_in)
    out = pl.pallas_call(
        weight_grad_kernel,
        out_shape=[shape(768, 512) for _ in range(8)],
        in_specs=[SMEM] + [ANY] * len(args),
        out_specs=[ANY] * 8,
        scratch_shapes=[
            pltpu.VMEM((ROWS, D), BF),
            pltpu.VMEM((ROWS, D), BF),
            pltpu.VMEM((ROWS, UNITS), BF),
            pltpu.VMEM((ROWS, 2 * UNITS), BF),
            pltpu.VMEM((D, 2 * UNITS), BF),
            pltpu.VMEM((UNITS, D), BF),
            pltpu.VMEM((UNITS, ROWS), BF),
            pltpu.SemaphoreType.DMA((96,)),
        ],
        compiler_params=pltpu.CompilerParams(**PARAMS),
        cost_estimate=cost(6 * ROWS * D * UNITS, 15e6),
    )(co, *args)
    return out[:4], out[4:]


def input_grad_kernel(co, *refs):
    grads_in, w_own, w_other, outs = refs[0], refs[1:5], refs[5:9], refs[9:13]
    grads, wide, result, sems = refs[13:]
    gate_up, _ = weight_copies(co, w_own, w_other, wide, None)
    started = run_copies([(grads_in, grads)] + gate_up, sems)
    wait_all(started)

    @pl.loop(0, 8)
    def _(n):
        block = spot(n, 256)
        result[:, block] = dot(grads[...], wide[block, :], NT).astype(BF)

    y, z = co[2], co[5]
    copies = []
    for o, y_off in enumerate(OFFS):
        yd = lax.rem(y + y_off + 4, 4)
        for n, off in enumerate(ZOFFS):
            to = lax.rem(z + off + 8, 8)
            src = result.at[spot(lax.rem(to, 4), HALF), spot(yd * 2 + to // 4, 256)]
            copies.append((src, outs[o].at[pl.ds(n * HALF, HALF), :]))
    wait_all(run_copies(copies, sems, len(started)))


def input_grad_call(co, grads, w_own, w_other):
    args = (grads, *w_own, *w_other)
    return pl.pallas_call(
        input_grad_kernel,
        out_shape=[shape(8 * HALF, 256) for _ in range(4)],
        in_specs=[SMEM] + [ANY] * len(args),
        out_specs=[ANY] * 4,
        scratch_shapes=[
            pltpu.VMEM((ROWS, 2 * UNITS), BF),
            pltpu.VMEM((D, 2 * UNITS), BF),
            pltpu.VMEM((ROWS, D), BF),
            pltpu.SemaphoreType.DMA((64,)),
        ],
        compiler_params=pltpu.CompilerParams(**PARAMS),
        cost_estimate=cost(4 * ROWS * D * UNITS, 10e6),
    )(co, *args)


def gather_z(value, last_rows):
    up = down = value
    pieces = [value]
    for _ in range(3):
        up, down = shift_z(up, 1), shift_z(down, -1)
        pieces += [up, down]
    half = last_rows // 2
    return pieces + [shift_z(up[:half], 1), shift_z(down[half:last_rows], -1)]


def add(*terms):
    total = terms[0].astype(F32)
    for term in terms[1:]:
        total = total + term.astype(F32)
    return total.astype(BF)


def scatter_z(pieces):
    up, down = shift_z(pieces[7], 1), shift_z(pieces[8], -1)
    half = up.shape[0]
    up = jnp.concatenate([add(pieces[5][:half], up), pieces[5][half:]])
    down = jnp.concatenate([pieces[6][:half], add(pieces[6][half:], down)])
    up, down = shift_z(up, 1), shift_z(down, -1)
    up, down = add(pieces[3], up), add(pieces[4], down)
    up, down = shift_z(up, 1), shift_z(down, -1)
    up, down = add(pieces[1], up), add(pieces[2], down)
    up, down = shift_z(up, 1), shift_z(down, -1)
    return add(pieces[0], up, down)


def split_cores(value, c):
    away = lax.dynamic_slice_in_dim(value, (1 - c) * HALF, HALF, 0)
    kept = lax.dynamic_slice_in_dim(value, c * HALF, HALF, 0)
    got = swap(away)
    return jnp.where(c == 0, jnp.concatenate([kept, got], 1), jnp.concatenate([got, kept], 1))


def join_cores(value, c):
    away = lax.dynamic_slice_in_dim(value, (1 - c) * 128, 128, 1)
    kept = lax.dynamic_slice_in_dim(value, c * 128, 128, 1)
    got = swap(away)
    return jnp.where(c == 0, jnp.concatenate([kept, got], 0), jnp.concatenate([got, kept], 0))


def local(tokens, cotangent, prefix, gate_weight, up_weight, down_weight):
    x, zl, y, zh, c = (lax.axis_index(a) for a in ("x", "zl", "y", "zh", "c"))
    co = jnp.stack([x, zl, y, zh, c, zh * 4 + zl, x, x]).astype(jnp.int32)

    sent = move(
        pack_kernel, 12, co, gate_weight, up_weight, down_weight, out_shape=[shape(128, 768) for _ in range(3)]
    )
    tok = split_cores(tokens, c)
    cot = split_cores(cotangent, c)
    got = [shift(v, "zl", off) for v, off in zip(sent, OFFS[1:])]

    mine = lax.dynamic_slice_in_dim(prefix, c, 2).astype(BF)
    limits = jnp.broadcast_to(jnp.pad(mine, (0, 14))[:, None], (16, 256))
    tok_y = [tok] + [shift(tok, "y", off) for off in OFFS[1:]]
    tok_in = gather_z(jnp.concatenate(tok_y + [limits]), ROWS)
    cot_z = gather_z(cot, HALF)
    cot_own = jnp.concatenate(cot_z)
    cot_in = [cot_own] + [shift(cot_own, "y", off) for off in OFFS[1:]]

    placed = move(
        place_kernel, 12, co, gate_weight, up_weight, down_weight, *got, out_shape=shape(768, 512)
    )
    w_own = [placed] + [shift(placed, "x", off) for off in OFFS[1:]]
    w_other = [swap(v) for v in w_own]

    hid, grads, mixed_terms = hidden_call(co, tok_in, cot_in, w_own, w_other)
    own_terms, other_terms = weight_grad_call(co, hid, grads, tok_in, cot_in)
    back_terms = input_grad_call(co, grads, w_own, w_other)

    mixed_z = scatter_z(mixed_terms)
    parts = [mixed_z[o * HALF : (o + 1) * HALF] for o in range(4)]
    mixed = join_cores(add(parts[0], *[shift(p, "y", off) for p, off in zip(parts[1:], OFFS[1:])]), c)

    chip_terms = [add(a, swap(b)) for a, b in zip(own_terms, other_terms)]
    total = add(chip_terms[0], *[shift(p, "x", off) for p, off in zip(chip_terms[1:], OFFS[1:])])

    back_y = add(back_terms[0], *[shift(p, "y", off) for p, off in zip(back_terms[1:], OFFS[1:])])
    pieces = [back_y[n * HALF : (n + 1) * HALF] for n in range(8)]
    pieces = pieces[:7] + [pieces[7][: HALF // 2], pieces[7][HALF // 2 :]]
    input_grad = join_cores(scatter_z(pieces), c)

    sent = move(pack_back_kernel, 9, co, total, out_shape=[shape(128, 768) for _ in range(3)])
    got = [shift(v, "zl", off) for v, off in zip(sent, OFFS[1:])]
    gate_grad, up_grad, down_grad = move(
        place_back_kernel,
        15,
        co,
        total,
        *got,
        out_shape=[shape(128, 1024), shape(128, 1024), shape(1024, 128)],
    )
    return mixed, input_grad, gate_grad, up_grad, down_grad


def solution(mesh):
    fine = Mesh(mesh.devices.reshape(4, 4, 4, 2, 2), ("x", "zl", "y", "zh", "c"))
    rows, columns = ("x", "zl"), ("y", "zh", "c")
    return jax.shard_map(
        local,
        mesh=fine,
        in_specs=(
            P(rows, columns),
            P(rows, columns),
            P(rows),
            P(rows, columns),
            P(rows, columns),
            P(columns, rows),
        ),
        out_specs=(
            P(rows, columns),
            P(rows, columns),
            P(rows, columns),
            P(rows, columns),
            P(columns, rows),
        ),
        check_vma=False,
    )
```

time: 939 us -> 387 us (0.41)
  waiting for transfers between devices: 847 us -> 136 us
  Pallas kernels: 0 us -> 126 us
  starting transfers between devices: 0.58 us -> 90.1 us
  matrix products: 40.3 us -> 0 us
  local copies, waits for them, and re-layouts: 32.8 us -> 16.3 us
  between operations: 14.2 us -> 1.52 us
  other arithmetic: 0.01 us -> 11.7 us
    unnamed x15 -> x0, waiting for transfers between devices: 426 us -> none
    all_gather x5 -> x0, waiting for transfers between devices: 420 us -> none  [the longest x1 109 us: local(): down_full = lax.all_gather(down_weight, 'dp', axis=1, tiled=True)]
    ppermute x0 -> x68, waiting for transfers between devices: none -> 136 us  [the longest x24 100 us: shift(): return lax.ppermute(value, axis, [(i, (i + by) % 4) for i in range(4)])]
    pallas_call x0 -> x7, Pallas kernels: none -> 126 us  [the longest x4 90.9 us: move(): pl.pallas_call(kernel, out_shape=out_shape, in_specs=[SMEM] + [ANY] * len...]
    ppermute x0 -> x68, starting transfers between devices: none -> 90.1 us  [the longest x32 57.5 us: shift_z(): return lax.ppermute(value, ('zl', 'zh'), pairs)]
    dot_general x9 -> x0, matrix products: 40.3 us -> none  [the longest x1 7.43 us: local_terms(): lax.dot_general(cotangent_rows, down_full, (((1,), (1,)), ((), ())), pref...]
    unnamed x28 -> x78, local copies, waits for them, and re-layouts: 32.8 us -> 13.1 us
    convert_element_type x0 -> x19, other arithmetic: none -> 10.2 us  [the longest x18 9.47 us: add(): return total.astype(BF)]
  transfers between devices with their start and end apart: 10 -> 68, of which waited for: 10 -> 28; matrix products, arithmetic and copies ran while one was open for 6% -> 4% of each run, Pallas kernels for 0% -> 23%
where the time goes in v1:
time: 387 us; the launch traced here: 382 us
  waiting for transfers between devices  136 us (35%)
  Pallas kernels  126 us (33%)
  starting transfers between devices  90.1 us (23%)
  local copies, waits for them, and re-layouts  16.3 us (4%)
  other arithmetic  11.7 us (3%)
    ppermute x24, waiting for transfers between devices, shift(): return lax.ppermute(value, axis, [(i, (i + by) % 4) for i in range(4)])  100 us
    pallas_call x4, Pallas kernels, move(): pl.pallas_call(kernel, out_shape=out_shape, in_specs=[SMEM] + [ANY] * len...  90.9 us
    ppermute x32, starting transfers between devices, shift_z(): return lax.ppermute(value, ('zl', 'zh'), pairs)  57.5 us
    ppermute x32, waiting for transfers between devices, shift_z(): return lax.ppermute(value, ('zl', 'zh'), pairs)  36 us
    ppermute x24, starting transfers between devices, shift(): return lax.ppermute(value, axis, [(i, (i + by) % 4) for i in range(4)])  29.9 us
    pallas_call x1, Pallas kernels, hidden_call(): pl.pallas_call(hidden_kernel, out_shape=outs, in_specs=[SMEM] + [ANY] * l...  14.2 us
    pallas_call x1, Pallas kernels, weight_grad_call(): pl.pallas_call(weight_grad_kernel, out_shape=[shape(768, 512) for _ in ra...  13.1 us
    unnamed x78, local copies, waits for them, and re-layouts  13.1 us
  transfers between devices with their start and end apart: 68, of which 28 were waited for; matrix products, arithmetic and copies ran while one was open for 4% of the time, Pallas kernels for 23%

profile of v1, /device:TPU:10, one launch (start us, length us, event | category | flops | bytes accessed | tf_op | source)
XLA Modules:
  0.0 381.8 jit_solution(16005857122337095428)
XLA Ops:
  19.5 19.7 %shard_map.101 = (bf16[128,768]{1,0:T(8,128)(2,1)}, bf16[128,768]{1,0:T(8,128)(2,1)}, bf16[128,768]{1,0:T(8,128)(2,1)}) custom-call(s32[8]{0:T(128)} %stack.29.co, bf16[128,1024]{1,0:T(8,128)(2,1)} %gate.3, bf16[128,1024]{1,0:T(8,128)(2,1)} %up.3, bf16[1024,128]{1,0:T(8,128)(2,1)} %down.3), custom_call_target="tpu_custom_call" | custom-call | bytes 786432 | tf_op jit(solution)/shard_map/pallas_call | solution.py:132
  39.3 3.9 %collective-permute-start.25 = (bf16[128,768]{1,0:T(8,128)(2,1)}, bf16[128,768]{1,0:T(8,128)(2,1)S(1)}, u32[]{:S(2)}, u32[]{:S(2)}) collective-permute-start(bf16[128,768]{1,0:T(8,128)(2,1)} %get-tuple-element.38), channel_id=1, source_target_pairs={{0,48},{16,0},{32,16},{48,32},{1,49},{17,1},{33,17},{49,33},{2,50}... | collective-permute-start | bytes 589832 | tf_op jit(solution)/shard_map/ppermute | solution.py:27
  49.3 6.7 %collective-permute-start.15 = (bf16[192,256]{1,0:T(8,128)(2,1)S(1)}, bf16[192,256]{1,0:T(8,128)(2,1)S(1)}, u32[]{:S(2)}, u32[]{:S(2)}) collective-permute-start(bf16[192,256]{1,0:T(8,128)(2,1)S(1)} %collective-permute-done.13), channel_id=1, source_target_pairs={{0,16},{16,32},{32,48},{48,2},{2,18},{18,34},{34,50},{50,0},{1,17}... | collective-permute-start | bytes 294920 | tf_op jit(solution)/shard_map/ppermute | solution.py:35
  56.1 3.9 %collective-permute-done.26.rest_2_ = bf16[128,768]{1,0:T(8,128)(2,1)S(1)} collective-permute-done((bf16[128,768]{1,0:T(8,128)(2,1)}, bf16[128,768]{1,0:T(8,128)(2,1)S(1)}, u32[]{:S(2)}, u32[]{:S(2)}) %collective-permute-start.26) | collective-permute-done | bytes 196640 | tf_op jit(solution)/shard_map/ppermute | solution.py:27
  60.7 25.7 %shard_map.102.refs_13_.refs_1_ = bf16[768,512]{1,0:T(8,128)(2,1)} custom-call(s32[8]{0:T(128)} %stack.29.co, bf16[128,1024]{1,0:T(8,128)(2,1)} %gate.3, bf16[128,1024]{1,0:T(8,128)(2,1)} %up.3, bf16[1024,128]{1,0:T(8,128)(2,1)} %down.3, bf16[128,768]{1,0:T(8,128)(2,1)} %copy-done.27, bf16[128,768]{1,0:T(8,128)(2,1)} %copy-done.29, bf16[128,768]{1,0:T(8,128)(2,1)} %copy-done.32), custom_call_target="tpu_custom_call" | custom-call | bytes 1376256 | tf_op jit(solution)/shard_map/pallas_call | solution.py:132
  91.7 3.3 collective-permute-done.17
  102.5 3.9 %collective-permute-done.20 = bf16[96,256]{1,0:T(8,128)(2,1)S(1)} collective-permute-done((bf16[96,256]{1,0:T(8,128)(2,1)S(1)}, bf16[96,256]{1,0:T(8,128)(2,1)S(1)}, u32[]{:S(2)}, u32[]{:S(2)}) %collective-permute-start.20) | collective-permute-done | bytes 49184 | tf_op jit(solution)/shard_map/ppermute | solution.py:35
  110.1 4.0 %collective-permute-done.28.refs_15_.refs_3_ = bf16[768,512]{1,0:T(8,128)(2,1)S(1)} collective-permute-done((bf16[768,512]{1,0:T(8,128)(2,1)}, bf16[768,512]{1,0:T(8,128)(2,1)S(1)}, u32[]{:S(2)}, u32[]{:S(2)}) %collective-permute-start.28) | collective-permute-done | bytes 786464 | tf_op jit(solution)/shard_map/ppermute | solution.py:27
  114.2 13.5 %collective-permute-done.29.refs_16_.refs_4_ = bf16[768,512]{1,0:T(8,128)(2,1)S(1)} collective-permute-done((bf16[768,512]{1,0:T(8,128)(2,1)}, bf16[768,512]{1,0:T(8,128)(2,1)S(1)}, u32[]{:S(2)}, u32[]{:S(2)}) %collective-permute-start.29) | collective-permute-done | bytes 786464 | tf_op jit(solution)/shard_map/ppermute | solution.py:27
  130.2 17.2 %collective-permute-done.22.refs_11_.refs_13_ = bf16[1536,256]{1,0:T(8,128)(2,1)S(1)} collective-permute-done((bf16[1536,256]{1,0:T(8,128)(2,1)S(1)}, bf16[1536,256]{1,0:T(8,128)(2,1)S(1)}, u32[]{:S(2)}, u32[]{:S(2)}) %collective-permute-start.22) | collective-permute-done | bytes 786464 | tf_op jit(solution)/shard_map/ppermute | solution.py:27
  147.5 12.3 %collective-permute-done.23.refs_12_.refs_14_ = bf16[1536,256]{1,0:T(8,128)(2,1)S(1)} collective-permute-done((bf16[1536,256]{1,0:T(8,128)(2,1)S(1)}, bf16[1536,256]{1,0:T(8,128)(2,1)S(1)}, u32[]{:S(2)}, u32[]{:S(2)}) %collective-permute-start.23) | collective-permute-done | bytes 786464 | tf_op jit(solution)/shard_map/ppermute | solution.py:27
  159.8 10.3 %collective-permute-start.11 = (bf16[384,256]{1,0:T(8,128)(2,1)S(1)}, bf16[384,256]{1,0:T(8,128)(2,1)S(1)}, u32[]{:S(2)}, u32[]{:S(2)}) collective-permute-start(bf16[384,256]{1,0:T(8,128)(2,1)S(1)} %slice.102), channel_id=1, source_target_pairs={{0,50},{16,0},{32,16},{48,32},{2,48},{18,2},{34,18},{50,34},{1,51}... | collective-permute-start | bytes 589832 | tf_op jit(solution)/shard_map/ppermute | solution.py:35
  170.1 3.9 %collective-permute-done.11.refs_8_.refs_10_ = bf16[384,256]{1,0:T(8,128)(2,1)S(1)} collective-permute-done((bf16[384,256]{1,0:T(8,128)(2,1)S(1)}, bf16[384,256]{1,0:T(8,128)(2,1)S(1)}, u32[]{:S(2)}, u32[]{:S(2)}) %collective-permute-start.11) | collective-permute-done | bytes 196640 | tf_op jit(solution)/shard_map/ppermute | solution.py:35
  177.2 14.2 %shard_map.103 = (bf16[768,512]{1,0:T(8,128)(2,1)S(1)}, bf16[768,1024]{1,0:T(8,128)(2,1)}, bf16[768,256]{1,0:T(8,128)(2,1)S(1)}, bf16[768,256]{1,0:T(8,128)(2,1)...) custom-call(s32[8]{0:T(128)S(1)} %copy-done.1, ...), custom_call_target="tpu_custom_call" | custom-call | flops 6442450944 | bytes 18000000 | tf_op jit(solution)/shard_map/pallas_call | solution.py:263
  202.5 8.1 %shard_map.104 = (bf16[1536,256]{1,0:T(8,128)(2,1)S(1)}, bf16[1536,256]{1,0:T(8,128)(2,1)S(1)}, bf16[1536,256]{1,0:T(8,128)(2,1)S(1)}, bf16[1536,256]{1,0:T(8,128)(2,1)S(1)}) custom-call(s32[8]{0:T(128)S(1)} %copy-done.1, bf16[768,1024]{1,0:T(8,128)(2,1)} %get-tuple-element.49.refs_0_.refs_1_, bf16[768,512]{1,0:T(8,128)(2,1)S(1)} %copy-done, ...), custom_call_target="tpu_custom_call" | custom-call | flops 3221225472 | bytes 10000000 | tf_op jit(solution)/shard_map/pallas_call | solution.py:372
  210.7 4.6 %collective-permute-start.48 = (bf16[1536,256]{1,0:T(8,128)(2,1)S(1)}, bf16[1536,256]{1,0:T(8,128)(2,1)S(1)}, u32[]{:S(2)}, u32[]{:S(2)}) collective-permute-start(bf16[1536,256]{1,0:T(8,128)(2,1)S(1)} %get-tuple-element.53), channel_id=1, source_target_pairs={{0,8},{4,12},{8,0},{12,4},{1,9},{5,13},{9,1},{13,5},{2,10},{6,14},... | collective-permute-start | bytes 2359304 | tf_op jit(solution)/shard_map/ppermute | solution.py:27
  217.3 3.7 collective-permute-start.39
  221.3 13.1 %shard_map.105 = (bf16[768,512]{1,0:T(8,128)(2,1)S(1)}, bf16[768,512]{1,0:T(8,128)(2,1)S(1)}, bf16[768,512]{1,0:T(8,128)(2,1)S(1)}, bf16[768,512]{1,0:T(8,128)(2...) custom-call(s32[8]{0:T(128)S(1)} %copy-done.1, ...), custom_call_target="tpu_custom_call" | custom-call | flops 4831838208 | bytes 15000000 | tf_op jit(solution)/shard_map/pallas_call | solution.py:326
  235.5 7.8 %collective-permute-done.47 = bf16[1536,256]{1,0:T(8,128)(2,1)S(1)} collective-permute-done((bf16[1536,256]{1,0:T(8,128)(2,1)S(1)}, bf16[1536,256]{1,0:T(8,128)(2,1)S(1)}, u32[]{:S(2)}, u32[]{:S(2)}) %collective-permute-start.47) | collective-permute-done | bytes 786464 | tf_op jit(solution)/shard_map/ppermute | solution.py:27
  251.3 5.5 %collective-permute-done.50 = bf16[192,256]{1,0:T(8,128)(2,1)S(1)} collective-permute-done((bf16[192,256]{1,0:T(8,128)(2,1)S(1)}, bf16[192,256]{1,0:T(8,128)(2,1)S(1)}, u32[]{:S(2)}, u32[]{:S(2)}) %collective-permute-start.50) | collective-permute-done | bytes 98336 | tf_op jit(solution)/shard_map/ppermute | solution.py:35
  262.9 4.4 %collective-permute-done.36 = bf16[768,256]{1,0:T(8,128)(2,1)S(1)} collective-permute-done((bf16[768,256]{1,0:T(8,128)(2,1)S(1)}, bf16[768,256]{1,0:T(8,128)(2,1)S(1)}, u32[]{:S(2)}, u32[]{:S(2)}) %collective-permute-start.36) | collective-permute-done | bytes 393248 | tf_op jit(solution)/shard_map/ppermute | solution.py:35
  267.6 3.3 collective-permute-start.41
  273.4 3.3 collective-permute-start.55
  279.0 4.3 %collective-permute-done.37 = bf16[768,256]{1,0:T(8,128)(2,1)S(1)} collective-permute-done((bf16[768,256]{1,0:T(8,128)(2,1)S(1)}, bf16[768,256]{1,0:T(8,128)(2,1)S(1)}, u32[]{:S(2)}, u32[]{:S(2)}) %collective-permute-start.37) | collective-permute-done | bytes 393248 | tf_op jit(solution)/shard_map/ppermute | solution.py:35
  292.1 3.4 collective-permute-done.43
  296.5 3.8 collective-permute-done.42
  301.9 11.1 %collective-permute-done.62 = bf16[768,512]{1,0:T(8,128)(2,1)} collective-permute-done((bf16[768,512]{1,0:T(8,128)(2,1)}, bf16[768,512]{1,0:T(8,128)(2,1)}, u32[]{:S(2)}, u32[]{:S(2)}) %collective-permute-start.62) | collective-permute-done | bytes 786464 | tf_op jit(solution)/shard_map/ppermute | solution.py:27
  316.0 19.7 %shard_map.106 = (bf16[128,768]{1,0:T(8,128)(2,1)}, bf16[128,768]{1,0:T(8,128)(2,1)}, bf16[128,768]{1,0:T(8,128)(2,1)}) custom-call(s32[8]{0:T(128)} %stack.29.co, bf16[768,512]{1,0:T(8,128)(2,1)} %add_convert_fusion.total), custom_call_target="tpu_custom_call" | custom-call | bytes 786432 | tf_op jit(solution)/shard_map/pallas_call | solution.py:132
  335.9 3.8 collective-permute-start.66
  341.0 4.6 %collective-permute-done.65.rest_0_ = bf16[128,768]{1,0:T(8,128)(2,1)S(1)} collective-permute-done((bf16[128,768]{1,0:T(8,128)(2,1)}, bf16[128,768]{1,0:T(8,128)(2,1)S(1)}, u32[]{:S(2)}, u32[]{:S(2)}) %collective-permute-start.65) | collective-permute-done | bytes 196640 | tf_op jit(solution)/shard_map/ppermute | solution.py:27
  348.1 7.1 %collective-permute-done.67.rest_2_ = bf16[128,768]{1,0:T(8,128)(2,1)S(1)} collective-permute-done((bf16[128,768]{1,0:T(8,128)(2,1)}, bf16[128,768]{1,0:T(8,128)(2,1)S(1)}, u32[]{:S(2)}, u32[]{:S(2)}) %collective-permute-start.67) | collective-permute-done | bytes 196640 | tf_op jit(solution)/shard_map/ppermute | solution.py:27
  355.9 25.7 %shard_map.107 = (bf16[128,1024]{1,0:T(8,128)(2,1)}, bf16[128,1024]{1,0:T(8,128)(2,1)}, bf16[1024,128]{1,0:T(8,128)(2,1)}) custom-call(s32[8]{0:T(128)} %stack.29.co, bf16[768,512]{1,0:T(8,128)(2,1)} %add_convert_fusion.total, bf16[128,768]{1,0:T(8,128)(2,1)} %copy-done.28, bf16[128,768]{1,0:T(8,128)(2,1)} %copy-done.30, bf16[128,768]{1,0:T(8,128)(2,1)} %copy-done.31), custom_call_target="tpu_custom_call" | custom-call | bytes 1376256 | tf_op jit(solution)/shard_map/pallas_call | solution.py:132
  (232 shorter events, 100.2 us)
Async XLA Ops:
  12.8 75.2 %collective-permute-start.4 = (bf16[784,256]{1,0:T(8,128)(2,1)S(1)}, bf16[784,256]{1,0:T(8,128)(2,1)S(1)}, u32[]{:S(2)}, u32[]{:S(2)}) collective-permute-start(bf16[784,256]{1,0:T(8,128)(2,1)S(1)} %constant_dynamic-update-slice_fusion.refs_0_.refs_2_), channel_id=1, source_target_pairs={{0,16},{16,32},{32,48},{48,2},{2,18},{18,34},{34,50},{50,0},{1,17}... | collective-permute-start | bytes 1204232 | tf_op jit(solution)/shard_map/ppermute | solution.py:35
  14.7 28.5 %collective-permute-start.13 = (bf16[192,256]{1,0:T(8,128)(2,1)S(1)}, bf16[192,256]{1,0:T(8,128)(2,1)S(1)}, u32[]{:S(2)}, u32[]{:S(2)}) collective-permute-start(bf16[192,256]{1,0:T(8,128)(2,1)S(1)} %get-tuple-element.70), channel_id=1, source_target_pairs={{0,16},{16,32},{32,48},{48,2},{2,18},{18,34},{34,50},{50,0},{1,17}... | collective-permute-start | bytes 294920 | tf_op jit(solution)/shard_map/ppermute | solution.py:35
  16.7 27.0 %collective-permute-start.14 = (bf16[192,256]{1,0:T(8,128)(2,1)S(1)}, bf16[192,256]{1,0:T(8,128)(2,1)S(1)}, u32[]{:S(2)}, u32[]{:S(2)}) collective-permute-start(bf16[192,256]{1,0:T(8,128)(2,1)S(1)} %get-tuple-element.70), channel_id=1, source_target_pairs={{0,50},{16,0},{32,16},{48,32},{2,48},{18,2},{34,18},{50,34},{1,51}... | collective-permute-start | bytes 294920 | tf_op jit(solution)/shard_map/ppermute | solution.py:35
  43.7 54.1 %collective-permute-start.5 = (bf16[784,256]{1,0:T(8,128)(2,1)S(1)}, bf16[784,256]{1,0:T(8,128)(2,1)S(1)}, u32[]{:S(2)}, u32[]{:S(2)}) collective-permute-start(bf16[784,256]{1,0:T(8,128)(2,1)S(1)} %constant_dynamic-update-slice_fusion.refs_0_.refs_2_), channel_id=1, source_target_pairs={{0,50},{16,0},{32,16},{48,32},{2,48},{18,2},{34,18},{50,34},{1,51}... | collective-permute-start | bytes 1204232 | tf_op jit(solution)/shard_map/ppermute | solution.py:35
  49.3 38.7 %collective-permute-start.15 = (bf16[192,256]{1,0:T(8,128)(2,1)S(1)}, bf16[192,256]{1,0:T(8,128)(2,1)S(1)}, u32[]{:S(2)}, u32[]{:S(2)}) collective-permute-start(bf16[192,256]{1,0:T(8,128)(2,1)S(1)} %collective-permute-done.13), channel_id=1, source_target_pairs={{0,16},{16,32},{32,48},{48,2},{2,18},{18,34},{34,50},{50,0},{1,17}... | collective-permute-start | bytes 294920 | tf_op jit(solution)/shard_map/ppermute | solution.py:35
  56.0 32.7 %collective-permute-start.16 = (bf16[192,256]{1,0:T(8,128)(2,1)S(1)}, bf16[192,256]{1,0:T(8,128)(2,1)S(1)}, u32[]{:S(2)}, u32[]{:S(2)}) collective-permute-start(bf16[192,256]{1,0:T(8,128)(2,1)S(1)} %collective-permute-done.14), channel_id=1, source_target_pairs={{0,50},{16,0},{32,16},{48,32},{2,48},{18,2},{34,18},{50,34},{1,51}... | collective-permute-start | bytes 294920 | tf_op jit(solution)/shard_map/ppermute | solution.py:35
  86.4 21.7 %collective-permute-start.27 = (bf16[768,512]{1,0:T(8,128)(2,1)}, bf16[768,512]{1,0:T(8,128)(2,1)S(1)}, u32[]{:S(2)}, u32[]{:S(2)}) collective-permute-start(bf16[768,512]{1,0:T(8,128)(2,1)} %shard_map.102.refs_13_.refs_1_), channel_id=1, source_target_pairs={{0,64},{64,128},{128,192},{192,0},{1,65},{65,129},{129,193},{193,1... | collective-permute-start | bytes 2359304 | tf_op jit(solution)/shard_map/ppermute | solution.py:27
  88.0 19.5 %collective-permute-start.6 = (bf16[784,256]{1,0:T(8,128)(2,1)S(1)}, bf16[784,256]{1,0:T(8,128)(2,1)S(1)}, u32[]{:S(2)}, u32[]{:S(2)}) collective-permute-start(bf16[784,256]{1,0:T(8,128)(2,1)S(1)} %collective-permute-done.4.refs_1_.refs_3_), channel_id=1, source_target_pairs={{0,16},{16,32},{32,48},{48,2},{2,18},{18,34},{34,50},{50,0},{1,17}... | collective-permute-start | bytes 1204232 | tf_op jit(solution)/shard_map/ppermute | solution.py:35
  94.9 19.2 %collective-permute-start.28 = (bf16[768,512]{1,0:T(8,128)(2,1)}, bf16[768,512]{1,0:T(8,128)(2,1)S(1)}, u32[]{:S(2)}, u32[]{:S(2)}) collective-permute-start(bf16[768,512]{1,0:T(8,128)(2,1)} %shard_map.102.refs_13_.refs_1_), channel_id=1, source_target_pairs={{0,192},{64,0},{128,64},{192,128},{1,193},{65,1},{129,65},{193,129... | collective-permute-start | bytes 2359304 | tf_op jit(solution)/shard_map/ppermute | solution.py:27
  106.4 21.3 %collective-permute-start.29 = (bf16[768,512]{1,0:T(8,128)(2,1)}, bf16[768,512]{1,0:T(8,128)(2,1)S(1)}, u32[]{:S(2)}, u32[]{:S(2)}) collective-permute-start(bf16[768,512]{1,0:T(8,128)(2,1)} %shard_map.102.refs_13_.refs_1_), channel_id=1, source_target_pairs={{0,128},{64,192},{128,0},{192,64},{1,129},{65,193},{129,1},{193,65... | collective-permute-start | bytes 2359304 | tf_op jit(solution)/shard_map/ppermute | solution.py:27
  107.5 20.8 %collective-permute-start.30 = (bf16[768,512]{1,0:T(8,128)(2,1)}, bf16[768,512]{1,0:T(8,128)(2,1)S(1)}, u32[]{:S(2)}, u32[]{:S(2)}) collective-permute-start(bf16[768,512]{1,0:T(8,128)(2,1)} %shard_map.102.refs_13_.refs_1_), channel_id=1, source_target_pairs={{0,1},{1,0},{2,3},{3,2},{4,5},{5,4},{6,7},{7,6},{8,9},{9,8},{10,11... | collective-permute-start | bytes 2359304 | tf_op jit(solution)/shard_map/ppermute | solution.py:39
  107.6 22.0 %collective-permute-start.21 = (bf16[1536,256]{1,0:T(8,128)(2,1)S(1)}, bf16[1536,256]{1,0:T(8,128)(2,1)S(1)}, u32[]{:S(2)}, u32[]{:S(2)}) collective-permute-start(bf16[1536,256]{1,0:T(8,128)(2,1)S(1)} %constant_dynamic-update-slice_fusion.5.refs_9_.refs_11_), channel_id=1, source_target_pairs={{0,4},{4,8},{8,12},{12,0},{1,5},{5,9},{9,13},{13,1},{2,6},{6,10},{... | collective-permute-start | bytes 2359304 | tf_op jit(solution)/shard_map/ppermute | solution.py:27
  108.1 21.5 %collective-permute-start.8 = (bf16[784,256]{1,0:T(8,128)(2,1)S(1)}, bf16[784,256]{1,0:T(8,128)(2,1)S(1)}, u32[]{:S(2)}, u32[]{:S(2)}) collective-permute-start(bf16[784,256]{1,0:T(8,128)(2,1)S(1)} %collective-permute-done.6.refs_3_.refs_5_), channel_id=1, source_target_pairs={{0,16},{16,32},{32,48},{48,2},{2,18},{18,34},{34,50},{50,0},{1,17}... | collective-permute-start | bytes 1204232 | tf_op jit(solution)/shard_map/ppermute | solution.py:35
  127.7 19.8 %collective-permute-start.22 = (bf16[1536,256]{1,0:T(8,128)(2,1)S(1)}, bf16[1536,256]{1,0:T(8,128)(2,1)S(1)}, u32[]{:S(2)}, u32[]{:S(2)}) collective-permute-start(bf16[1536,256]{1,0:T(8,128)(2,1)S(1)} %constant_dynamic-update-slice_fusion.5.refs_9_.refs_11_), channel_id=1, source_target_pairs={{0,12},{4,0},{8,4},{12,8},{1,13},{5,1},{9,5},{13,9},{2,14},{6,2},{... | collective-permute-start | bytes 2359304 | tf_op jit(solution)/shard_map/ppermute | solution.py:27
  128.3 31.5 %collective-permute-start.23 = (bf16[1536,256]{1,0:T(8,128)(2,1)S(1)}, bf16[1536,256]{1,0:T(8,128)(2,1)S(1)}, u32[]{:S(2)}, u32[]{:S(2)}) collective-permute-start(bf16[1536,256]{1,0:T(8,128)(2,1)S(1)} %constant_dynamic-update-slice_fusion.5.refs_9_.refs_11_), channel_id=1, source_target_pairs={{0,8},{4,12},{8,0},{12,4},{1,9},{5,13},{9,1},{13,5},{2,10},{6,14},... | collective-permute-start | bytes 2359304 | tf_op jit(solution)/shard_map/ppermute | solution.py:27
  129.6 44.5 %collective-permute-start.31 = (bf16[768,512]{1,0:T(8,128)(2,1)S(1)}, bf16[768,512]{1,0:T(8,128)(2,1)S(1)}, u32[]{:S(2)}, u32[]{:S(2)}) collective-permute-start(bf16[768,512]{1,0:T(8,128)(2,1)S(1)} %collective-permute-done.27.refs_14_.refs_2_), channel_id=1, source_target_pairs={{0,1},{1,0},{2,3},{3,2},{4,5},{5,4},{6,7},{7,6},{8,9},{9,8},{10,11... | collective-permute-start | bytes 2359304 | tf_op jit(solution)/shard_map/ppermute | solution.py:39
  129.6 44.5 %collective-permute-start.32 = (bf16[768,512]{1,0:T(8,128)(2,1)S(1)}, bf16[768,512]{1,0:T(8,128)(2,1)S(1)}, u32[]{:S(2)}, u32[]{:S(2)}) collective-permute-start(bf16[768,512]{1,0:T(8,128)(2,1)S(1)} %collective-permute-done.28.refs_15_.refs_3_), channel_id=1, source_target_pairs={{0,1},{1,0},{2,3},{3,2},{4,5},{5,4},{6,7},{7,6},{8,9},{9,8},{10,11... | collective-permute-start | bytes 2359304 | tf_op jit(solution)/shard_map/ppermute | solution.py:39
  130.1 44.0 %collective-permute-start.33 = (bf16[768,512]{1,0:T(8,128)(2,1)S(1)}, bf16[768,512]{1,0:T(8,128)(2,1)S(1)}, u32[]{:S(2)}, u32[]{:S(2)}) collective-permute-start(bf16[768,512]{1,0:T(8,128)(2,1)S(1)} %collective-permute-done.29.refs_16_.refs_4_), channel_id=1, source_target_pairs={{0,1},{1,0},{2,3},{3,2},{4,5},{5,4},{6,7},{7,6},{8,9},{9,8},{10,11... | collective-permute-start | bytes 2359304 | tf_op jit(solution)/shard_map/ppermute | solution.py:39
  147.5 22.7 %collective-permute-start.10 = (bf16[384,256]{1,0:T(8,128)(2,1)S(1)}, bf16[384,256]{1,0:T(8,128)(2,1)S(1)}, u32[]{:S(2)}, u32[]{:S(2)}) collective-permute-start(bf16[384,256]{1,0:T(8,128)(2,1)S(1)} %slice.101), channel_id=1, source_target_pairs={{0,16},{16,32},{32,48},{48,2},{2,18},{18,34},{34,50},{50,0},{1,17}... | collective-permute-start | bytes 589832 | tf_op jit(solution)/shard_map/ppermute | solution.py:35
  191.4 25.8 %collective-permute-start.38 = (bf16[384,256]{1,0:T(8,128)(2,1)S(1)}, bf16[384,256]{1,0:T(8,128)(2,1)S(1)}, u32[]{:S(2)}, u32[]{:S(2)}) collective-permute-start(bf16[384,256]{1,0:T(8,128)(2,1)S(1)} %get-tuple-element.48), channel_id=1, source_target_pairs={{0,50},{16,0},{32,16},{48,32},{2,48},{18,2},{34,18},{50,34},{1,51}... | collective-permute-start | bytes 589832 | tf_op jit(solution)/shard_map/ppermute | solution.py:35
  194.5 26.6 %collective-permute-start.34 = (bf16[384,256]{1,0:T(8,128)(2,1)S(1)}, bf16[384,256]{1,0:T(8,128)(2,1)S(1)}, u32[]{:S(2)}, u32[]{:S(2)}) collective-permute-start(bf16[384,256]{1,0:T(8,128)(2,1)S(1)} %get-tuple-element.44), channel_id=1, source_target_pairs={{0,16},{16,32},{32,48},{48,2},{2,18},{18,34},{34,50},{50,0},{1,17}... | collective-permute-start | bytes 589832 | tf_op jit(solution)/shard_map/ppermute | solution.py:35
  210.7 24.7 %collective-permute-start.48 = (bf16[1536,256]{1,0:T(8,128)(2,1)S(1)}, bf16[1536,256]{1,0:T(8,128)(2,1)S(1)}, u32[]{:S(2)}, u32[]{:S(2)}) collective-permute-start(bf16[1536,256]{1,0:T(8,128)(2,1)S(1)} %get-tuple-element.53), channel_id=1, source_target_pairs={{0,8},{4,12},{8,0},{12,4},{1,9},{5,13},{9,1},{13,5},{2,10},{6,14},... | collective-permute-start | bytes 2359304 | tf_op jit(solution)/shard_map/ppermute | solution.py:27
  215.2 28.0 %collective-permute-start.47 = (bf16[1536,256]{1,0:T(8,128)(2,1)S(1)}, bf16[1536,256]{1,0:T(8,128)(2,1)S(1)}, u32[]{:S(2)}, u32[]{:S(2)}) collective-permute-start(bf16[1536,256]{1,0:T(8,128)(2,1)S(1)} %get-tuple-element.52), channel_id=1, source_target_pairs={{0,12},{4,0},{8,4},{12,8},{1,13},{5,1},{9,5},{13,9},{2,14},{6,2},{... | collective-permute-start | bytes 2359304 | tf_op jit(solution)/shard_map/ppermute | solution.py:27
  215.2 28.0 %collective-permute-start.46 = (bf16[1536,256]{1,0:T(8,128)(2,1)S(1)}, bf16[1536,256]{1,0:T(8,128)(2,1)S(1)}, u32[]{:S(2)}, u32[]{:S(2)}) collective-permute-start(bf16[1536,256]{1,0:T(8,128)(2,1)S(1)} %get-tuple-element.51), channel_id=1, source_target_pairs={{0,4},{4,8},{8,12},{12,0},{1,5},{5,9},{9,13},{13,1},{2,6},{6,10},{... | collective-permute-start | bytes 2359304 | tf_op jit(solution)/shard_map/ppermute | solution.py:27
  234.6 38.7 %collective-permute-start.61 = (bf16[768,512]{1,0:T(8,128)(2,1)S(1)}, bf16[768,512]{1,0:T(8,128)(2,1)S(1)}, u32[]{:S(2)}, u32[]{:S(2)}) collective-permute-start(bf16[768,512]{1,0:T(8,128)(2,1)S(1)} %get-tuple-element.60), channel_id=1, source_target_pairs={{0,1},{1,0},{2,3},{3,2},{4,5},{5,4},{6,7},{7,6},{8,9},{9,8},{10,11... | collective-permute-start | bytes 2359304 | tf_op jit(solution)/shard_map/ppermute | solution.py:39
  235.3 48.9 %collective-permute-start.59 = (bf16[768,512]{1,0:T(8,128)(2,1)S(1)}, bf16[768,512]{1,0:T(8,128)(2,1)S(1)}, u32[]{:S(2)}, u32[]{:S(2)}) collective-permute-start(bf16[768,512]{1,0:T(8,128)(2,1)S(1)} %get-tuple-element.58), channel_id=1, source_target_pairs={{0,1},{1,0},{2,3},{3,2},{4,5},{5,4},{6,7},{7,6},{8,9},{9,8},{10,11... | collective-permute-start | bytes 2359304 | tf_op jit(solution)/shard_map/ppermute | solution.py:39
  243.2 58.1 %collective-permute-start.58 = (bf16[768,512]{1,0:T(8,128)(2,1)S(1)}, bf16[768,512]{1,0:T(8,128)(2,1)S(1)}, u32[]{:S(2)}, u32[]{:S(2)}) collective-permute-start(bf16[768,512]{1,0:T(8,128)(2,1)S(1)} %get-tuple-element.56), channel_id=1, source_target_pairs={{0,1},{1,0},{2,3},{3,2},{4,5},{5,4},{6,7},{7,6},{8,9},{9,8},{10,11... | collective-permute-start | bytes 2359304 | tf_op jit(solution)/shard_map/ppermute | solution.py:39
  278.9 23.0 %collective-permute-start.64 = (bf16[768,512]{1,0:T(8,128)(2,1)}, bf16[768,512]{1,0:T(8,128)(2,1)}, u32[]{:S(2)}, u32[]{:S(2)}) collective-permute-start(bf16[768,512]{1,0:T(8,128)(2,1)} %add_convert_fusion.1), channel_id=1, source_target_pairs={{0,128},{64,192},{128,0},{192,64},{1,129},{65,193},{129,1},{193,65... | collective-permute-start | bytes 2359304 | tf_op jit(solution)/shard_map/ppermute | solution.py:27
  287.8 25.3 %collective-permute-start.62 = (bf16[768,512]{1,0:T(8,128)(2,1)}, bf16[768,512]{1,0:T(8,128)(2,1)}, u32[]{:S(2)}, u32[]{:S(2)}) collective-permute-start(bf16[768,512]{1,0:T(8,128)(2,1)} %add_convert_fusion.2), channel_id=1, source_target_pairs={{0,192},{64,0},{128,64},{192,128},{1,193},{65,1},{129,65},{193,129... | collective-permute-start | bytes 2359304 | tf_op jit(solution)/shard_map/ppermute | solution.py:27
  288.1 25.0 %collective-permute-start.60 = (bf16[768,512]{1,0:T(8,128)(2,1)}, bf16[768,512]{1,0:T(8,128)(2,1)}, u32[]{:S(2)}, u32[]{:S(2)}) collective-permute-start(bf16[768,512]{1,0:T(8,128)(2,1)} %add_convert_fusion.3), channel_id=1, source_target_pairs={{0,64},{64,128},{128,192},{192,0},{1,65},{65,129},{129,193},{193,1... | collective-permute-start | bytes 2359304 | tf_op jit(solution)/shard_map/ppermute | solution.py:27
  300.3 39.3 %collective-permute-start.57 = (bf16[192,128]{1,0:T(8,128)(2,1)S(1)}, bf16[192,128]{1,0:T(8,128)(2,1)S(1)}, u32[]{:S(2)}, u32[]{:S(2)}) collective-permute-start(bf16[192,128]{1,0:T(8,128)(2,1)S(1)} %get-tuple-element.85), channel_id=1, source_target_pairs={{0,1},{1,0},{2,3},{3,2},{4,5},{5,4},{6,7},{7,6},{8,9},{9,8},{10,11... | collective-permute-start | bytes 147464 | tf_op jit(solution)/shard_map/ppermute | solution.py:39
  301.3 39.0 %collective-permute-start.45 = (bf16[192,128]{1,0:T(8,128)(2,1)S(1)}, bf16[192,128]{1,0:T(8,128)(2,1)S(1)}, u32[]{:S(2)}, u32[]{:S(2)}) collective-permute-start(bf16[192,128]{1,0:T(8,128)(2,1)S(1)} %get-tuple-element.87), channel_id=1, source_target_pairs={{0,1},{1,0},{2,3},{3,2},{4,5},{5,4},{6,7},{7,6},{8,9},{9,8},{10,11... | collective-permute-start | bytes 147464 | tf_op jit(solution)/shard_map/ppermute | solution.py:39
  (70 other events, 1149.9 us)
